TPU v7x, 768 devices: a whole 4x8x12 slice. The times are simulated.
768 devices in a mesh: ray: 96 (over z, y), mp: 8 (over x, core).
Axes of the slice: x: 4, y: 8, z: 12, core: 2. Of those that a mesh axis runs over, the one named last changes fastest.
Arguments:
- ray_matrix: bfloat16 [3072, 32, 128, 128], P('ray', 'mp'), as said below
- block_cols: int32 [3072, 32], P('ray', 'mp'), may hold values from 0 to 95, as said below
- iterate: float32 [8, 96, 16, 128], P('mp', 'ray'), may hold values from -6 to 6
- residual: float32 [3072, 16, 128], P('ray'), may hold values from -6 to 6
Outputs:
- iterate_next: float32 [8, 96, 16, 128], P('mp', 'ray')
- residual_next: float32 [3072, 16, 128], P('ray')
Inputs may be any that keep to these rules, and one draw needn't show every extreme that they name: `block_cols`: slot k of a ray block belongs to model group k // 4; every model block of every group is named by at least one ray block. `ray_matrix`: all entries are positive path lengths.
All inputs are finite; a program needn't handle non-finite values.
Results may differ from a plain program's by a relative error of at most 0.00045.
Values may be sent and summed in bfloat16 or wider, within the bound.
A program may use at most 32 MiB of HBM per device.

v0:
```python
import jax
import jax.numpy as jnp
from jax import lax
from jax.sharding import PartitionSpec as P

eps = 1e-06


def local(ray_matrix, block_cols, iterate, residual):
    blocks_here = ray_matrix.shape[0]
    slots_here = ray_matrix.shape[1]
    block_len = ray_matrix.shape[2]
    rhs_count = residual.shape[1]
    model_here = iterate.shape[1]
    ray_count = lax.axis_size("ray")
    group_len = model_here * ray_count
    rows_low = residual.astype(jnp.bfloat16)
    unit_row = jnp.ones((blocks_here, 1, block_len), jnp.bfloat16)
    stacked = jnp.concatenate([rows_low, unit_row], axis=1)
    slot_terms = jnp.einsum(
        "rktc,rht->rkhc", ray_matrix, stacked, preferred_element_type=jnp.float32
    )
    flat_cols = block_cols.reshape(-1)
    partial_sum = jax.ops.segment_sum(
        slot_terms.reshape(blocks_here * slots_here, rhs_count + 1, block_len),
        flat_cols,
        num_segments=group_len,
    )
    offset_own = lax.axis_index("ray") * model_here
    summed = lax.psum(partial_sum, "ray")
    scaled_all = summed[:, :rhs_count] / summed[:, rhs_count:]
    direction_low = scaled_all.astype(jnp.bfloat16)
    own_sum = lax.dynamic_slice_in_dim(summed, offset_own, model_here, 0)
    own_scaled = lax.dynamic_slice_in_dim(scaled_all, offset_own, model_here, 0)
    gradient = own_sum[:, :rhs_count]
    grad_part = jnp.sum(gradient * own_scaled, axis=(0, 2))
    grad_norm = lax.psum(grad_part, ("ray", "mp"))
    picked = direction_low[block_cols]
    image_part = jnp.einsum(
        "rktc,rkhc->rht", ray_matrix, picked, preferred_element_type=jnp.float32
    )
    image_full = lax.psum(image_part.astype(jnp.bfloat16), "mp").astype(jnp.float32)
    image_sq = jnp.sum(image_full * image_full, axis=(0, 2))
    image_norm = lax.psum(image_sq, "ray")
    step_len = grad_norm / (image_norm + eps)
    iterate_next = iterate + step_len[None, None, :, None] * own_scaled[None]
    residual_next = residual - step_len[None, :, None] * image_full
    return (iterate_next, residual_next)


def solution(mesh):
    in_specs = (
        P("ray", "mp", None, None),
        P("ray", "mp"),
        P("mp", "ray", None, None),
        P("ray", None, None),
    )
    out_specs = (P("mp", "ray", None, None), P("ray", None, None))
    return jax.shard_map(local, mesh=mesh, in_specs=in_specs, out_specs=out_specs, check_vma=False)
```

profile of v0, /device:TPU:8, one launch (start us, length us, event | category | flops | bytes accessed | tf_op | source)
XLA Modules:
  0.0 670.0 jit_solution(14132820943755818573)
XLA Ops:
  7.2 0.0 all-reduce.4.cloned.1.call-start
  7.2 0.8 copy.8
  8.0 0.1 reshape.51
  8.1 1.0 convert_element_type.12
  9.1 2.9 fusion.3
  11.9 0.1 broadcast_in_dim.12
  12.0 0.0 copy-start.3
  12.0 5.6 scatter_fusion
  17.6 0.0 copy-start
  17.6 1.0 copy-done
  18.6 0.0 all-reduce.4.cloned.1.call-update
  18.7 0.0 all-reduce.6.cloned.1.call-start
  18.7 0.0 copy-done.3
  18.7 0.1 copy.9
  18.8 0.1 reshape.43
  19.0 243.1 %all-reduce.4.cloned.1.call-done = f32[96,17,128]{2,1,0:T(8,128)} async-done(((f32[96,17,128]{2,1,0:T(8,128)}), f32[96,17,128]{2,1,0:T(8,128)}) %all-reduce.4.cloned.1.call-update) | async-done | bytes 835600 | tf_op jit(solution)/shard_map/psum | solution.py:30
  262.1 1.0 slice.15
  263.1 1.3 fusion.9
  264.4 0.7 gather_fusion
  265.1 0.0 copy-start.2
  265.1 0.0 copy-start.1
  265.1 4.1 fusion
  269.2 0.0 all-reduce.6.cloned.1.call-update
  269.2 0.8 fusion.6
  270.0 72.3 %all-reduce.6.cloned.1.call-done = bf16[32,16,128]{2,1,0:T(8,128)(2,1)} async-done(((bf16[32,16,128]{2,1,0:T(8,128)(2,1)}), bf16[32,16,128]{2,1,0:T(8,128)(2,1)}) %all-reduce.6.cloned.1.call-update) | async-done | bytes 131088 | tf_op jit(solution)/shard_map/psum | solution.py:42
  342.4 1.1 fusion.1
  343.4 107.6 %psum.29 = f32[16]{0:T(128)S(1)} all-reduce(f32[16]{0:T(128)S(1)} %fusion.6), channel_id=1, replica_groups=mesh['ray'=96,'mp'=8] {'ray','mp'}, use_global_device_ids=true, to_apply=%region_3.0 | all-reduce | flops 16 | bytes 128 | tf_op jit(solution)/shard_map/psum | solution.py:37
  451.1 209.7 %psum.31 = f32[16]{0:T(128)S(1)} all-reduce(f32[16]{0:T(128)S(1)} %fusion.1), channel_id=1, replica_groups=mesh['ray'=96,'mp'=8] {'ray'}, use_global_device_ids=true, to_apply=%region_6.0 | all-reduce | flops 16 | bytes 128 | tf_op jit(solution)/shard_map/psum | solution.py:44
  660.8 0.0 copy-done.2
  660.8 0.7 fusion.7
  661.5 0.0 copy-done.1
  661.5 1.7 fusion.2
  (3 shorter events, 0.0 us)
Async XLA Ops:
  7.2 254.9 %all-reduce.4.cloned.1.call-start = ((), (), s32[]{:S(2)}) async-start(), calls=%async_computation | async-start | bytes 2359296 | tf_op jit(solution)/shard_map/psum | solution.py:30
  12.0 6.7 %copy-start.3 = (s32[32,4]{0,1:T(4,128)S(1)}, s32[32,4]{0,1:T(4,128)}, u32[]{:S(2)}) copy-start(s32[32,4]{0,1:T(4,128)} %param.5) | copy-start | bytes 1540
  17.6 1.1 copy-start
  18.7 323.7 %all-reduce.6.cloned.1.call-start = ((), (), s32[]{:S(2)}) async-start(), calls=%async_computation.1 | async-start | bytes 262144 | tf_op jit(solution)/shard_map/psum | solution.py:42
  265.1 395.8 %copy-start.2 = (f32[1,1,16,128]{3,2,1,0:T(8,128)S(1)}, f32[1,1,16,128]{3,2,1,0:T(8,128)}, u32[]{:S(2)}) copy-start(f32[1,1,16,128]{3,2,1,0:T(8,128)} %param.6) | copy-start | bytes 24580
  265.1 396.4 %copy-start.1 = (f32[32,16,128]{2,1,0:T(8,128)S(1)}, f32[32,16,128]{2,1,0:T(8,128)}, u32[]{:S(2)}) copy-start(f32[32,16,128]{2,1,0:T(8,128)} %param.7) | copy-start | bytes 786436
Sparse Core Ops, SparseCore 0:
  18.8 243.2 all-reduce.3
  269.3 72.9 all-reduce.5
where the time goes:
time: 670 us
  blocking collectives  317 us (47%)
  waiting for transfers between devices  315 us (47%)
  between operations  14.1 us (2%)
  other arithmetic  12.1 us (2%)
  matrix products  6.94 us (1%)
    psum x1, waiting for transfers between devices, local(): summed = lax.psum(partial_sum, 'ray')  243 us
    psum x1, blocking collectives, local(): image_norm = lax.psum(image_sq, 'ray')  210 us
    psum x1, blocking collectives, local(): grad_norm = lax.psum(grad_part, ('ray', 'mp'))  108 us
    psum x1, waiting for transfers between devices, local(): lax.psum(image_part.astype(jnp.bfloat16), 'mp').astype(jnp.float32)  72.3 us
  transfers between devices with their start and end apart: 2, of which 2 were waited for; matrix products, arithmetic and copies ran while one was open for 0% of the time, Pallas kernels for 0%

commit v1 on v0

v1 whole, which is shorter than its diff:
```python
import functools
import jax
import jax.numpy as jnp
from jax import lax
from jax.experimental import pallas as pl
from jax.experimental.pallas import tpu as pltpu
from jax.sharding import PartitionSpec as P

MESH = pl.DeviceIdType.MESH
F32 = jnp.float32
BF16 = jnp.bfloat16
eps = 1e-06

NY = 8
H_Y = 10
H_Z = 7
CHUNKS = 8


def kernel(nz, nmp, a_hbm, cols_s, cols_v, it_hbm, res_hbm, itn_ref, resn_ref,
           a_v, res_v, it_v, terms, gy, gz, ry, rz, s2y, s2z, ry2, rz2, grad_v, scaled_v,
           dirs, img_f, img_b, ri, img, nsrc, nz_r, ny_r, nmp_r,
           a_sem, res_sem, it_sem,
           sy, sz, vy, vz, sy2, sz2, vy2, vz2, sa1, va1, sa2, va2,
           si, vi, sg, vg, sn1, vn1, sn2, vn2, sn3, vn3):
    ny = NY
    mb = nz * ny
    rb = a_v.shape[0]
    rb_own = rb // nmp
    per = rb // CHUNKS
    me = lax.axis_index("ray")
    mp = lax.axis_index("mp")
    z = me // ny
    y = me % ny
    y_of = [None] + [(y + d) % ny for d in range(1, ny)]
    z_of = [None] + [(z + d) % nz for d in range(1, nz)]
    mp_of = [None] + [(mp + d) % nmp for d in range(1, nmp)]
    y_id = lambda d: (z * ny + y_of[d], mp)
    z_id = lambda d: (z_of[d] * ny + y, mp)
    mp_id = lambda d: (me, mp_of[d])

    barrier = pltpu.get_barrier_semaphore()
    for d in range(1, nz):
        pl.semaphore_signal(barrier, inc=1, device_id=z_id(d), device_id_type=MESH)
    for d in range(1, ny):
        pl.semaphore_signal(barrier, inc=1, device_id=y_id(d), device_id_type=MESH)
    for d in range(1, nmp):
        pl.semaphore_signal(barrier, inc=1, device_id=mp_id(d), device_id_type=MESH)

    res_copy = pltpu.make_async_copy(res_hbm, res_v, res_sem)
    res_copy.start()
    a_copies = []
    for i in range(CHUNKS):
        part = pl.ds(i * per, per)
        copy = pltpu.make_async_copy(a_hbm.at[part], a_v.at[part], a_sem.at[i])
        copy.start()
        a_copies.append(copy)
    it_copy = pltpu.make_async_copy(it_hbm, it_v, it_sem)
    it_copy.start()

    sends = []

    def push(src, dst, send_sem, recv_sem, target):
        copy = pltpu.make_async_remote_copy(
            src_ref=src, dst_ref=dst, send_sem=send_sem, recv_sem=recv_sem,
            device_id=target, device_id_type=MESH)
        copy.start()
        sends.append(copy)
        return copy

    lane = lax.broadcasted_iota(jnp.int32, (rb, 128), 1)
    slots = cols_v.shape[1]

    def one_hot(place):
        parts = [(place(cols_v[:, k:k + 1]) == lane).astype(F32) for k in range(slots)]
        hot = jnp.concatenate(parts, axis=0).T[:mb].astype(BF16)
        return jnp.concatenate([hot, hot, hot], axis=1)

    hot_z = one_hot(lambda c: c)
    hot_y = one_hot(lambda c: (c % ny) * nz + c // ny)

    tiles = rb * slots
    res_copy.wait()
    ones = jnp.ones((16, 128), BF16)
    for i in range(CHUNKS):
        a_copies[i].wait()

        def products(j, carry):
            r = i * per + j
            left = jnp.concatenate([res_v[r].astype(BF16), ones], axis=0)
            right = jnp.concatenate([a_v[r, k] for k in range(slots)], axis=1)
            out = jnp.dot(left, right, preferred_element_type=F32)
            for k in range(slots):
                terms[pl.ds(k * rb + r, 24, stride=tiles), :] = out[:24, k * 128:(k + 1) * 128]
            return carry

        lax.fori_loop(0, per, products, 0, unroll=True)

    def split(h):
        t = terms[pl.ds(h * tiles, tiles), :]
        hi = t.astype(BF16)
        rest = t - hi.astype(F32)
        mid = rest.astype(BF16)
        low = (rest - mid.astype(F32)).astype(BF16)
        return jnp.concatenate([hi, mid, low], axis=0)

    def segment(hot, dst, rows, first):
        for h in range(0, rows, 2):
            n = min(2, rows - h)
            right = jnp.concatenate([split(first + h + i) for i in range(n)], axis=1)
            out = jnp.dot(hot, right, preferred_element_type=F32)
            for i in range(n):
                dst[pl.ds(h + i, mb, stride=rows), :] = out[:, i * 128:(i + 1) * 128]

    segment(hot_z, gz, H_Z, H_Y)
    pl.semaphore_wait(barrier, nz + ny + nmp - 3)
    len_z = ny * H_Z
    len_y = nz * H_Y
    rs_z = [push(gz.at[pl.ds(z_of[d] * len_z, len_z)], rz.at[d - 1], sz.at[d - 1], vz.at[d - 1], z_id(d))
            for d in range(1, nz)]
    segment(hot_y, gy, H_Y, 0)
    rs_y = [push(gy.at[pl.ds(y_of[d] * len_y, len_y)], ry.at[d - 1], sy.at[d - 1], vy.at[d - 1], y_id(d))
            for d in range(1, ny)]

    acc_y = gy[pl.ds(pl.multiple_of(y * len_y, 8), len_y), :]
    for d in range(1, ny):
        rs_y[d - 1].wait_recv()
        acc_y = acc_y + ry[d - 1]
    for i in range(nz):
        s2y[i, 0:H_Y, :] = acc_y[i * H_Y:(i + 1) * H_Y]
    rs_y2 = [push(s2y.at[z_of[d]], ry2.at[d - 1], sy2.at[d - 1], vy2.at[d - 1], z_id(d))
             for d in range(1, nz)]
    acc_z = gz[pl.ds(pl.multiple_of(z * len_z, 8), len_z), :]
    for d in range(1, nz):
        rs_z[d - 1].wait_recv()
        acc_z = acc_z + rz[d - 1]
    for i in range(ny):
        s2z[i, 0:H_Z, :] = acc_z[i * H_Z:(i + 1) * H_Z]
    rs_z2 = [push(s2z.at[y_of[d]], rz2.at[d - 1], sz2.at[d - 1], vz2.at[d - 1], y_id(d))
             for d in range(1, ny)]

    sum_z = s2z[y]
    for d in range(1, ny):
        rs_z2[d - 1].wait_recv()
        sum_z = sum_z + rz2[d - 1]
    sum_y = s2y[z]
    for d in range(1, nz):
        rs_y2[d - 1].wait_recv()
        sum_y = sum_y + ry2[d - 1]
    grad_v[0:H_Y, :] = sum_y[0:H_Y]
    grad_v[H_Y:16, :] = sum_z[0:H_Z - 1]
    gradient = grad_v[...]
    scaled = gradient / sum_z[H_Z - 1:H_Z]
    scaled_v[...] = scaled

    own = y * nz + z
    dirs[own] = scaled.astype(BF16)
    ag1 = [push(dirs.at[own], dirs.at[own], sa1.at[d - 1], va1.at[d - 1], z_id(d)) for d in range(1, nz)]
    for copy in ag1:
        copy.wait_recv()
    row = pl.ds(y * nz, nz)
    ag2 = [push(dirs.at[row], dirs.at[row], sa2.at[d - 1], va2.at[d - 1], y_id(d)) for d in range(1, ny)]
    for copy in ag2:
        copy.wait_recv()

    def image_of(first):
        def one(j, carry):
            r = first + j
            picked = []
            for k in range(slots):
                c = cols_s[r, k]
                picked.append(dirs[(c % ny) * nz + c // ny])
            left = jnp.concatenate(picked, axis=1)
            right = jnp.concatenate([a_v[r, k] for k in range(slots)], axis=1)
            out = lax.dot_general(left, right, (((1,), (1,)), ((), ())), preferred_element_type=F32)
            img_f[r] = out
            img_b[r] = out.astype(BF16)
            return carry

        lax.fori_loop(0, rb_own, one, 0, unroll=True)

    rs_i = []
    for d in range(1, nmp):
        first = mp_of[d] * rb_own
        image_of(first)
        rs_i.append(push(img_b.at[pl.ds(first, rb_own)], ri.at[d - 1], si.at[d - 1], vi.at[d - 1], mp_id(d)))
    mine = pl.ds(mp * rb_own, rb_own)
    image_of(mp * rb_own)
    total = img_f[mine]
    for d in range(1, nmp):
        rs_i[d - 1].wait_recv()
        total = total + ri[d - 1].astype(F32)
    img[mine] = total

    squares = jnp.concatenate(
        [jnp.sum(total * total, axis=0), gradient * scaled, jnp.zeros((96, 128), F32)], axis=0)
    nsrc[0] = jnp.sum(squares.T, axis=0, keepdims=True)
    n1 = [push(nsrc.at[0], nz_r.at[d - 1], sn1.at[d - 1], vn1.at[d - 1], z_id(d)) for d in range(1, nz)]
    ag_i = [push(img.at[mine], img.at[mine], sg.at[d - 1], vg.at[d - 1], mp_id(d)) for d in range(1, nmp)]
    it_copy.wait()
    acc = nsrc[0]
    for d in range(1, nz):
        n1[d - 1].wait_recv()
        acc = acc + nz_r[d - 1]
    nsrc[1] = acc
    n2 = [push(nsrc.at[1], ny_r.at[d - 1], sn2.at[d - 1], vn2.at[d - 1], y_id(d)) for d in range(1, ny)]
    for d in range(1, ny):
        n2[d - 1].wait_recv()
        acc = acc + ny_r[d - 1]
    nmp_r[mp] = acc
    n3 = [push(nmp_r.at[mp], nmp_r.at[mp], sn3.at[d - 1], vn3.at[d - 1], mp_id(d)) for d in range(1, nmp)]
    for copy in ag_i:
        copy.wait_recv()
    for copy in n3:
        copy.wait_recv()
    acc = nmp_r[0]
    for i in range(1, nmp):
        acc = acc + nmp_r[i]
    wide = jnp.broadcast_to(acc, (16, 128))
    sub = lax.broadcasted_iota(jnp.int32, (16, 128), 0)
    lane16 = lax.broadcasted_iota(jnp.int32, (16, 128), 1)
    image_norm = jnp.sum(jnp.where(lane16 == sub, wide, 0.0), axis=1, keepdims=True)
    grad_norm = jnp.sum(jnp.where(lane16 == sub + 16, wide, 0.0), axis=1, keepdims=True)
    step = grad_norm / (image_norm + eps)
    itn_ref[0, 0] = it_v[0, 0] + step * scaled_v[...]
    resn_ref[...] = res_v[...] - step[None] * img[...]
    for copy in sends:
        copy.wait_send()


def local(ray_matrix, block_cols, iterate, residual):
    nmp = lax.axis_size("mp")
    nz = lax.axis_size("ray") // NY
    rb, slots = block_cols.shape
    mb = nz * NY
    rb_own = rb // nmp
    vmem = lambda *shape: pltpu.VMEM(shape, F32)
    dma = lambda n: pltpu.SemaphoreType.DMA((n,))
    scratch = [
        pltpu.VMEM(ray_matrix.shape, BF16),
        pltpu.VMEM(residual.shape, F32),
        pltpu.VMEM(iterate.shape, F32),
        vmem(24 * rb * slots, 128),
        vmem(mb * H_Y, 128),
        vmem(mb * H_Z, 128),
        vmem(NY - 1, nz * H_Y, 128),
        vmem(nz - 1, NY * H_Z, 128),
        vmem(nz, 16, 128),
        vmem(NY, 8, 128),
        vmem(nz - 1, 16, 128),
        vmem(NY - 1, 8, 128),
        vmem(16, 128),
        vmem(16, 128),
        pltpu.VMEM((mb, 16, 128), BF16),
        vmem(rb, 16, 128),
        pltpu.VMEM((rb, 16, 128), BF16),
        pltpu.VMEM((nmp - 1, rb_own, 16, 128), BF16),
        vmem(rb, 16, 128),
        vmem(2, 1, 128),
        vmem(nz - 1, 1, 128),
        vmem(NY - 1, 1, 128),
        vmem(nmp, 1, 128),
        dma(CHUNKS), pltpu.SemaphoreType.DMA, pltpu.SemaphoreType.DMA,
    ]
    y, z, m = NY - 1, nz - 1, nmp - 1
    for n in (y, z, y, z, z, y, z, y, z, z, y, y, m, m, m, m, z, z, y, y, m, m):
        scratch.append(dma(n))
    any_spec = pl.BlockSpec(memory_space=pl.ANY)
    return pl.pallas_call(
        functools.partial(kernel, nz, nmp),
        out_shape=(
            jax.ShapeDtypeStruct(iterate.shape, F32),
            jax.ShapeDtypeStruct(residual.shape, F32),
        ),
        in_specs=[any_spec, pl.BlockSpec(memory_space=pltpu.SMEM), pl.BlockSpec(memory_space=pltpu.VMEM),
                  any_spec, any_spec],
        out_specs=(pl.BlockSpec(memory_space=pltpu.VMEM),) * 2,
        scratch_shapes=scratch,
        compiler_params=pltpu.CompilerParams(
            collective_id=0, has_side_effects=True, vmem_limit_bytes=48 * 2**20),
        cost_estimate=pl.CostEstimate(flops=300_000_000, bytes_accessed=5_000_000, transcendentals=0),
        name="cgls",
    )(ray_matrix, block_cols, block_cols, iterate, residual)


def solution(mesh):
    in_specs = (
        P("ray", "mp", None, None),
        P("ray", "mp"),
        P("mp", "ray", None, None),
        P("ray", None, None),
    )
    out_specs = (P("mp", "ray", None, None), P("ray", None, None))
    return jax.shard_map(local, mesh=mesh, in_specs=in_specs, out_specs=out_specs, check_vma=False)
```

time: 670 us -> 83.8 us (0.13)
  the two profiles are of different devices: /device:TPU:8 before, /device:TPU:1 now
where the time goes in v1:
time: 83.8 us; the launch traced here: 83.5 us
  Pallas kernels  77 us (92%)
  local copies, waits for them, and re-layouts  5.9 us (7%)
    pallas_call x1, Pallas kernels, local(): pl.pallas_call(functools.partial(kernel, nz, nmp), out_shape=(jax.ShapeDt...  77 us
    unnamed x9, local copies, waits for them, and re-layouts  5.9 us

profile of v1, /device:TPU:1, one launch (start us, length us, event | category | flops | bytes accessed | tf_op | source)
XLA Modules:
  0.0 83.5 jit_solution(14974878027886435561)
XLA Ops:
  0.6 0.8 copy.6.cols_s.cols_v
  1.4 0.0 copy-start
  1.4 2.2 %copy-done = bf16[32,4,128,128]{3,2,1,0:T(8,128)(2,1)S(1)} copy-done((bf16[32,4,128,128]{3,2,1,0:T(8,128)(2,1)S(1)}, bf16[32,4,128,128]{3,2,1,0:T(8,128)(2,1)}, u32[]{:S(2)}) %copy-start) | copy-done | bytes 4194328
  3.6 0.0 copy-start.1
  3.6 0.9 %copy-done.1 = f32[32,16,128]{2,1,0:T(8,128)S(1)} copy-done((f32[32,16,128]{2,1,0:T(8,128)S(1)}, f32[32,16,128]{2,1,0:T(8,128)}, u32[]{:S(2)}) %copy-start.1) | copy-done | bytes 262168
  4.5 0.0 copy-start.2
  4.5 0.7 copy-done.2
  5.2 77.0 %cgls.1 = (f32[1,1,16,128]{3,2,1,0:T(8,128)S(1)}, f32[32,16,128]{2,1,0:T(8,128)S(1)}) custom-call(bf16[32,4,128,128]{3,2,1,0:T(8,128)(2,1)S(1)} %copy-done, s32[32,4]{1,0:T(8,128)S(1)} %copy.6.cols_s.cols_v, s32[32,4]{1,0:T(8,128)S(1)} %copy.6.cols_s.cols_v, f32[1,1,16,128]{3,2,1,0:T(8,128)S(1)} %copy-done.2, f32[32,16,128]{2,1,0:T(8,128)S(1)} %copy-done.1), custom_call_target="tpu_custom_call" | custom-call | flops 300000000 | bytes 5000000 | tf_op jit(solution)/shard_map/cgls/pallas_call | solution.py:269
  82.2 0.6 copy.10
  82.8 0.7 copy.11
Async XLA Ops:
  1.4 2.2 %copy-start = (bf16[32,4,128,128]{3,2,1,0:T(8,128)(2,1)S(1)}, bf16[32,4,128,128]{3,2,1,0:T(8,128)(2,1)}, u32[]{:S(2)}) copy-start(bf16[32,4,128,128]{3,2,1,0:T(8,128)(2,1)} %a_hbm.1) | copy-start | bytes 12582916
  3.6 0.9 %copy-start.1 = (f32[32,16,128]{2,1,0:T(8,128)S(1)}, f32[32,16,128]{2,1,0:T(8,128)}, u32[]{:S(2)}) copy-start(f32[32,16,128]{2,1,0:T(8,128)} %res_hbm.1) | copy-start | bytes 786436
  4.5 0.7 copy-start.2

commit v2 on v1

--- a/solution.py
+++ b/solution.py
@@ -17,12 +17,12 @@
 CHUNKS = 8
 
 
-def kernel(nz, nmp, a_hbm, cols_s, cols_v, it_hbm, res_hbm, itn_ref, resn_ref,
-           a_v, res_v, it_v, terms, gy, gz, ry, rz, s2y, s2z, ry2, rz2, grad_v, scaled_v,
-           dirs, img_f, img_b, ri, img, nsrc, nz_r, ny_r, nmp_r,
-           a_sem, res_sem, it_sem,
+def kernel(nz, nmp, a_hbm, cols_hbm, it_hbm, res_hbm, itn_ref, resn_ref,
+           a_v, res_v, it_v, cols_v, cols_s, terms, gy, gz, ry, rz, s2y, s2z, ry2, rz2, grad_v, scaled_v,
+           dirs, img_f, img_b, ri, img, nsrc, n1_r, n2_r,
+           a_sem, res_sem, it_sem, cv_sem, cs_sem,
            sy, sz, vy, vz, sy2, sz2, vy2, vz2, sa1, va1, sa2, va2,
-           si, vi, sg, vg, sn1, vn1, sn2, vn2, sn3, vn3):
+           si, vi, sg, vg, sn1, vn1, sn2, vn2):
     ny = NY
     mb = nz * ny
     rb = a_v.shape[0]
@@ -39,6 +39,20 @@
     z_id = lambda d: (z_of[d] * ny + y, mp)
     mp_id = lambda d: (me, mp_of[d])
 
+    nx = nmp // 2
+    x = mp // 2
+    core = mp % 2
+    other_core = x * 2 + 1 - core
+
+    def zc_id(i):
+        if i < nz - 1:
+            return z_id(i + 1)
+        d = i - (nz - 1)
+        return (((z + d) % nz) * ny + y, other_core)
+
+    def yx_id(i):
+        return (z * ny + (y + i % ny) % ny, ((x + i // ny) % nx) * 2 + core)
+
     barrier = pltpu.get_barrier_semaphore()
     for d in range(1, nz):
         pl.semaphore_signal(barrier, inc=1, device_id=z_id(d), device_id_type=MESH)
@@ -46,7 +60,15 @@
         pl.semaphore_signal(barrier, inc=1, device_id=y_id(d), device_id_type=MESH)
     for d in range(1, nmp):
         pl.semaphore_signal(barrier, inc=1, device_id=mp_id(d), device_id_type=MESH)
-
+    for i in range(nz, 2 * nz - 1):
+        pl.semaphore_signal(barrier, inc=1, device_id=zc_id(i), device_id_type=MESH)
+    for i in range(ny, nx * ny):
+        if i % ny:
+            pl.semaphore_signal(barrier, inc=1, device_id=yx_id(i), device_id_type=MESH)
+    greeted = (nz - 1) + (ny - 1) + (nmp - 1) + (nz - 1) + (nx - 1) * (ny - 1)
+
+    cv_copy = pltpu.make_async_copy(cols_hbm, cols_v, cv_sem)
+    cv_copy.start()
     res_copy = pltpu.make_async_copy(res_hbm, res_v, res_sem)
     res_copy.start()
     a_copies = []
@@ -57,6 +79,8 @@
         a_copies.append(copy)
     it_copy = pltpu.make_async_copy(it_hbm, it_v, it_sem)
     it_copy.start()
+    cs_copy = pltpu.make_async_copy(cols_hbm, cols_s, cs_sem)
+    cs_copy.start()
 
     sends = []
 
@@ -68,14 +92,15 @@
         sends.append(copy)
         return copy
 
-    lane = lax.broadcasted_iota(jnp.int32, (rb, 128), 1)
-    slots = cols_v.shape[1]
+    block = lax.broadcasted_iota(jnp.int32, (mb, rb), 0)
+    slots = cols_v.shape[0]
 
     def one_hot(place):
-        parts = [(place(cols_v[:, k:k + 1]) == lane).astype(F32) for k in range(slots)]
-        hot = jnp.concatenate(parts, axis=0).T[:mb].astype(BF16)
+        parts = [(place(cols_v[k:k + 1, :]) == block).astype(F32) for k in range(slots)]
+        hot = jnp.concatenate(parts, axis=1).astype(BF16)
         return jnp.concatenate([hot, hot, hot], axis=1)
 
+    cv_copy.wait()
     hot_z = one_hot(lambda c: c)
     hot_y = one_hot(lambda c: (c % ny) * nz + c // ny)
 
@@ -113,7 +138,7 @@
                 dst[pl.ds(h + i, mb, stride=rows), :] = out[:, i * 128:(i + 1) * 128]
 
     segment(hot_z, gz, H_Z, H_Y)
-    pl.semaphore_wait(barrier, nz + ny + nmp - 3)
+    pl.semaphore_wait(barrier, greeted)
     len_z = ny * H_Z
     len_y = nz * H_Y
     rs_z = [push(gz.at[pl.ds(z_of[d] * len_z, len_z)], rz.at[d - 1], sz.at[d - 1], vz.at[d - 1], z_id(d))
@@ -128,7 +153,7 @@
         acc_y = acc_y + ry[d - 1]
     for i in range(nz):
         s2y[i, 0:H_Y, :] = acc_y[i * H_Y:(i + 1) * H_Y]
-    rs_y2 = [push(s2y.at[z_of[d]], ry2.at[d - 1], sy2.at[d - 1], vy2.at[d - 1], z_id(d))
+    rs_y2 = [push(s2y.at[z_of[d], pl.ds(0, H_Y)], ry2.at[d - 1, pl.ds(0, H_Y)], sy2.at[d - 1], vy2.at[d - 1], z_id(d))
              for d in range(1, nz)]
     acc_z = gz[pl.ds(pl.multiple_of(z * len_z, 8), len_z), :]
     for d in range(1, nz):
@@ -143,11 +168,11 @@
     for d in range(1, ny):
         rs_z2[d - 1].wait_recv()
         sum_z = sum_z + rz2[d - 1]
-    sum_y = s2y[z]
+    sum_y = s2y[z, 0:H_Y]
     for d in range(1, nz):
         rs_y2[d - 1].wait_recv()
-        sum_y = sum_y + ry2[d - 1]
-    grad_v[0:H_Y, :] = sum_y[0:H_Y]
+        sum_y = sum_y + ry2[d - 1, 0:H_Y]
+    grad_v[0:H_Y, :] = sum_y
     grad_v[H_Y:16, :] = sum_z[0:H_Z - 1]
     gradient = grad_v[...]
     scaled = gradient / sum_z[H_Z - 1:H_Z]
@@ -162,13 +187,15 @@
     ag2 = [push(dirs.at[row], dirs.at[row], sa2.at[d - 1], va2.at[d - 1], y_id(d)) for d in range(1, ny)]
     for copy in ag2:
         copy.wait_recv()
+
+    cs_copy.wait()
 
     def image_of(first):
         def one(j, carry):
             r = first + j
             picked = []
             for k in range(slots):
-                c = cols_s[r, k]
+                c = cols_s[k, r]
                 picked.append(dirs[(c % ny) * nz + c // ny])
             left = jnp.concatenate(picked, axis=1)
             right = jnp.concatenate([a_v[r, k] for k in range(slots)], axis=1)
@@ -195,27 +222,28 @@
     squares = jnp.concatenate(
         [jnp.sum(total * total, axis=0), gradient * scaled, jnp.zeros((96, 128), F32)], axis=0)
     nsrc[0] = jnp.sum(squares.T, axis=0, keepdims=True)
-    n1 = [push(nsrc.at[0], nz_r.at[d - 1], sn1.at[d - 1], vn1.at[d - 1], z_id(d)) for d in range(1, nz)]
+    n1 = [push(nsrc.at[0], n1_r.at[i], sn1.at[i], vn1.at[i], zc_id(i)) for i in range(2 * nz - 1)]
     ag_i = [push(img.at[mine], img.at[mine], sg.at[d - 1], vg.at[d - 1], mp_id(d)) for d in range(1, nmp)]
     it_copy.wait()
+    for copy in n1:
+        copy.wait_recv()
     acc = nsrc[0]
-    for d in range(1, nz):
-        n1[d - 1].wait_recv()
-        acc = acc + nz_r[d - 1]
-    nsrc[1] = acc
-    n2 = [push(nsrc.at[1], ny_r.at[d - 1], sn2.at[d - 1], vn2.at[d - 1], y_id(d)) for d in range(1, ny)]
-    for d in range(1, ny):
-        n2[d - 1].wait_recv()
-        acc = acc + ny_r[d - 1]
-    nmp_r[mp] = acc
-    n3 = [push(nmp_r.at[mp], nmp_r.at[mp], sn3.at[d - 1], vn3.at[d - 1], mp_id(d)) for d in range(1, nmp)]
+    for i in range(nz - 1):
+        acc = acc + n1_r[i]
+    other = n1_r[nz - 1]
+    for i in range(nz, 2 * nz - 1):
+        other = other + n1_r[i]
+    own_x = pl.ds(x * ny, 1)
+    n2_r[own_x] = (acc + other)[None]
+    n2 = [push(n2_r.at[own_x], n2_r.at[pl.ds(x * ny + i % ny, 1)], sn2.at[i - 1], vn2.at[i - 1], yx_id(i))
+          for i in range(1, nx * ny)]
     for copy in ag_i:
         copy.wait_recv()
-    for copy in n3:
-        copy.wait_recv()
-    acc = nmp_r[0]
-    for i in range(1, nmp):
-        acc = acc + nmp_r[i]
+    for copy in n2:
+        copy.wait_recv()
+    acc = n2_r[0]
+    for i in range(1, nx * ny):
+        acc = acc + n2_r[i]
     wide = jnp.broadcast_to(acc, (16, 128))
     sub = lax.broadcasted_iota(jnp.int32, (16, 128), 0)
     lane16 = lax.broadcasted_iota(jnp.int32, (16, 128), 1)
@@ -240,6 +268,8 @@
         pltpu.VMEM(ray_matrix.shape, BF16),
         pltpu.VMEM(residual.shape, F32),
         pltpu.VMEM(iterate.shape, F32),
+        pltpu.VMEM((slots, rb), jnp.int32),
+        pltpu.SMEM((slots, rb), jnp.int32),
         vmem(24 * rb * slots, 128),
         vmem(mb * H_Y, 128),
         vmem(mb * H_Z, 128),
@@ -256,14 +286,14 @@
         pltpu.VMEM((rb, 16, 128), BF16),
         pltpu.VMEM((nmp - 1, rb_own, 16, 128), BF16),
         vmem(rb, 16, 128),
-        vmem(2, 1, 128),
-        vmem(nz - 1, 1, 128),
-        vmem(NY - 1, 1, 128),
-        vmem(nmp, 1, 128),
-        dma(CHUNKS), pltpu.SemaphoreType.DMA, pltpu.SemaphoreType.DMA,
+        vmem(1, 1, 128),
+        vmem(2 * nz - 1, 1, 128),
+        vmem(nmp // 2 * NY, 1, 128),
+        dma(CHUNKS), *[pltpu.SemaphoreType.DMA] * 4,
     ]
     y, z, m = NY - 1, nz - 1, nmp - 1
-    for n in (y, z, y, z, z, y, z, y, z, z, y, y, m, m, m, m, z, z, y, y, m, m):
+    zc, yx = 2 * nz - 1, nmp // 2 * NY - 1
+    for n in (y, z, y, z, z, y, z, y, z, z, y, y, m, m, m, m, zc, zc, yx, yx):
         scratch.append(dma(n))
     any_spec = pl.BlockSpec(memory_space=pl.ANY)
     return pl.pallas_call(
@@ -272,15 +302,14 @@
             jax.ShapeDtypeStruct(iterate.shape, F32),
             jax.ShapeDtypeStruct(residual.shape, F32),
         ),
-        in_specs=[any_spec, pl.BlockSpec(memory_space=pltpu.SMEM), pl.BlockSpec(memory_space=pltpu.VMEM),
-                  any_spec, any_spec],
+        in_specs=[any_spec] * 4,
         out_specs=(pl.BlockSpec(memory_space=pltpu.VMEM),) * 2,
         scratch_shapes=scratch,
         compiler_params=pltpu.CompilerParams(
-            collective_id=0, has_side_effects=True, vmem_limit_bytes=48 * 2**20),
+            collective_id=0, has_side_effects=True, vmem_limit_bytes=61 * 2**20),
         cost_estimate=pl.CostEstimate(flops=300_000_000, bytes_accessed=5_000_000, transcendentals=0),
         name="cgls",
-    )(ray_matrix, block_cols, block_cols, iterate, residual)
+    )(ray_matrix, block_cols.T, iterate, residual)
 
 
 def solution(mesh):

time: 83.8 us -> 79.7 us (0.951)
  local copies, waits for them, and re-layouts: 5.9 us -> 2.96 us
  Pallas kernels: 77 us -> 75.8 us
    unnamed x9 -> x2, local copies, waits for them, and re-layouts: 5.9 us -> 2.96 us
    pallas_call x1, Pallas kernels: 77 us -> 75.8 us  [local(): pl.pallas_call(functools.partial(kernel, nz, nmp), out_shape=(jax.ShapeDt...]
where the time goes in v2:
time: 79.7 us; the launch traced here: 79.5 us
  Pallas kernels  75.8 us (95%)
  local copies, waits for them, and re-layouts  2.96 us (4%)
    pallas_call x1, Pallas kernels, local(): pl.pallas_call(functools.partial(kernel, nz, nmp), out_shape=(jax.ShapeDt...  75.8 us
    unnamed x2, local copies, waits for them, and re-layouts  2.96 us

profile of v2, /device:TPU:1, one launch (start us, length us, event | category | flops | bytes accessed | tf_op | source)
XLA Modules:
  0.0 79.5 jit_solution(17968071198753148685)
XLA Ops:
  0.6 75.8 %cgls.1 = (f32[1,1,16,128]{3,2,1,0:T(8,128)}, f32[32,16,128]{2,1,0:T(8,128)}) custom-call(bf16[32,4,128,128]{3,2,1,0:T(8,128)(2,1)} %a_hbm.1, s32[4,32]{1,0:T(4,128)} %bitcast.1, f32[1,1,16,128]{3,2,1,0:T(8,128)} %it_hbm.1, f32[32,16,128]{2,1,0:T(8,128)} %res_hbm.1), custom_call_target="tpu_custom_call" | custom-call | flops 300000000 | bytes 5000000 | tf_op jit(solution)/shard_map/cgls/pallas_call | solution.py:299
  76.5 1.3 %copy.8 = f32[1,1,16,128]{3,2,1,0:T(8,128)} copy(f32[1,1,16,128]{3,2,1,0:T(8,128)} %get-tuple-element.4) | data formatting | bytes 16384
  77.8 1.7 %copy.9 = f32[32,16,128]{2,1,0:T(8,128)} copy(f32[32,16,128]{2,1,0:T(8,128)} %get-tuple-element.5) | data formatting | bytes 524288

commit v3 on v2

--- a/solution.py
+++ b/solution.py
@@ -15,12 +15,21 @@
 H_Y = 10
 H_Z = 7
 CHUNKS = 8
-
-
-def kernel(nz, nmp, a_hbm, cols_hbm, it_hbm, res_hbm, itn_ref, resn_ref,
-           a_v, res_v, it_v, cols_v, cols_s, terms, gy, gz, ry, rz, s2y, s2z, ry2, rz2, grad_v, scaled_v,
+GROUPS = 3
+
+
+def far_first(n):
+    return sorted(range(1, n), key=lambda d: -min(d, n - d))
+
+
+def place_of(rel, n):
+    return n - 1 - 2 * rel if rel < n // 2 else 2 * rel - n
+
+
+def kernel(nz, nmp, a_hbm, cols_hbm, res_hbm, small_ref, img_hbm,
+           a_v, res_v, cols_v, place_v, place_s, terms, gy, gz, ry, rz, s2y, s2z, ry2, rz2, grad_v,
            dirs, img_f, img_b, ri, img, nsrc, n1_r, n2_r,
-           a_sem, res_sem, it_sem, cv_sem, cs_sem,
+           a_sem, res_sem, cv_sem, ps_sem, out_sem,
            sy, sz, vy, vz, sy2, sz2, vy2, vz2, sa1, va1, sa2, va2,
            si, vi, sg, vg, sn1, vn1, sn2, vn2):
     ny = NY
@@ -54,9 +63,9 @@
         return (z * ny + (y + i % ny) % ny, ((x + i // ny) % nx) * 2 + core)
 
     barrier = pltpu.get_barrier_semaphore()
-    for d in range(1, nz):
+    for d in far_first(nz):
         pl.semaphore_signal(barrier, inc=1, device_id=z_id(d), device_id_type=MESH)
-    for d in range(1, ny):
+    for d in far_first(ny):
         pl.semaphore_signal(barrier, inc=1, device_id=y_id(d), device_id_type=MESH)
     for d in range(1, nmp):
         pl.semaphore_signal(barrier, inc=1, device_id=mp_id(d), device_id_type=MESH)
@@ -77,10 +86,6 @@
         copy = pltpu.make_async_copy(a_hbm.at[part], a_v.at[part], a_sem.at[i])
         copy.start()
         a_copies.append(copy)
-    it_copy = pltpu.make_async_copy(it_hbm, it_v, it_sem)
-    it_copy.start()
-    cs_copy = pltpu.make_async_copy(cols_hbm, cols_s, cs_sem)
-    cs_copy.start()
 
     sends = []
 
@@ -101,8 +106,19 @@
         return jnp.concatenate([hot, hot, hot], axis=1)
 
     cv_copy.wait()
-    hot_z = one_hot(lambda c: c)
-    hot_y = one_hot(lambda c: (c % ny) * nz + c // ny)
+
+    def near(c, mine, n):
+        rel = c - mine
+        rel = jnp.where(rel < 0, rel + n, rel)
+        return jnp.where(rel < n // 2, n - 1 - 2 * rel, 2 * rel - n)
+
+    place_z = lambda c: (c // ny) * ny + near(c % ny, y, ny)
+    place_y = lambda c: (c % ny) * nz + near(c // ny, z, nz)
+    hot_z = one_hot(place_z)
+    hot_y = one_hot(place_y)
+    place_v[...] = place_y(cols_v[...])
+    place_copy = pltpu.make_async_copy(place_v, place_s, ps_sem)
+    place_copy.start()
 
     tiles = rb * slots
     res_copy.wait()
@@ -141,62 +157,84 @@
     pl.semaphore_wait(barrier, greeted)
     len_z = ny * H_Z
     len_y = nz * H_Y
-    rs_z = [push(gz.at[pl.ds(z_of[d] * len_z, len_z)], rz.at[d - 1], sz.at[d - 1], vz.at[d - 1], z_id(d))
-            for d in range(1, nz)]
+    rs_z = {d: push(gz.at[pl.ds(z_of[d] * len_z, len_z)], rz.at[d - 1], sz.at[d - 1], vz.at[d - 1], z_id(d))
+            for d in far_first(nz)}
     segment(hot_y, gy, H_Y, 0)
-    rs_y = [push(gy.at[pl.ds(y_of[d] * len_y, len_y)], ry.at[d - 1], sy.at[d - 1], vy.at[d - 1], y_id(d))
-            for d in range(1, ny)]
-
-    acc_y = gy[pl.ds(pl.multiple_of(y * len_y, 8), len_y), :]
-    for d in range(1, ny):
-        rs_y[d - 1].wait_recv()
-        acc_y = acc_y + ry[d - 1]
-    for i in range(nz):
-        s2y[i, 0:H_Y, :] = acc_y[i * H_Y:(i + 1) * H_Y]
-    rs_y2 = [push(s2y.at[z_of[d], pl.ds(0, H_Y)], ry2.at[d - 1, pl.ds(0, H_Y)], sy2.at[d - 1], vy2.at[d - 1], z_id(d))
-             for d in range(1, nz)]
+    len_g = len_y // GROUPS
+    places_g = nz // GROUPS
+    rs_y = {}
+    for g in range(GROUPS):
+        for d in far_first(ny):
+            i = (d - 1) * GROUPS + g
+            rs_y[d, g] = push(gy.at[pl.ds(y_of[d] * len_y + g * len_g, len_g)],
+                              ry.at[d - 1, pl.ds(g * len_g, len_g)], sy.at[i], vy.at[i], y_id(d))
+    rel_of = {place_of(rel, nz): rel for rel in range(nz)}
+    rs_y2 = {}
+
+    def sum_group(g):
+        part = gy[pl.ds(pl.multiple_of(y * len_y + g * len_g, 8), len_g), :]
+        for d in far_first(ny):
+            rs_y[d, g].wait_recv()
+        for d in range(1, ny):
+            part = part + ry[d - 1, g * len_g:(g + 1) * len_g]
+        for i in range(places_g):
+            place = g * places_g + i
+            s2y[place, 0:H_Y, :] = part[i * H_Y:(i + 1) * H_Y]
+            d = rel_of[place]
+            if d:
+                rs_y2[d] = push(s2y.at[place, pl.ds(0, H_Y)], ry2.at[d - 1, pl.ds(0, H_Y)],
+                                sy2.at[d - 1], vy2.at[d - 1], z_id(d))
+
+    for g in range(GROUPS - 1):
+        sum_group(g)
     acc_z = gz[pl.ds(pl.multiple_of(z * len_z, 8), len_z), :]
+    for d in far_first(nz):
+        rs_z[d].wait_recv()
     for d in range(1, nz):
-        rs_z[d - 1].wait_recv()
         acc_z = acc_z + rz[d - 1]
     for i in range(ny):
         s2z[i, 0:H_Z, :] = acc_z[i * H_Z:(i + 1) * H_Z]
-    rs_z2 = [push(s2z.at[y_of[d]], rz2.at[d - 1], sz2.at[d - 1], vz2.at[d - 1], y_id(d))
-             for d in range(1, ny)]
-
-    sum_z = s2z[y]
+    rs_z2 = {d: push(s2z.at[place_of(d, ny)], rz2.at[d - 1], sz2.at[d - 1], vz2.at[d - 1], y_id(d))
+             for d in far_first(ny)}
+    sum_group(GROUPS - 1)
+
+    sum_z = s2z[ny - 1]
     for d in range(1, ny):
-        rs_z2[d - 1].wait_recv()
+        rs_z2[d].wait_recv()
         sum_z = sum_z + rz2[d - 1]
-    sum_y = s2y[z, 0:H_Y]
+    sum_y = s2y[nz - 1, 0:H_Y]
     for d in range(1, nz):
-        rs_y2[d - 1].wait_recv()
+        rs_y2[d].wait_recv()
         sum_y = sum_y + ry2[d - 1, 0:H_Y]
     grad_v[0:H_Y, :] = sum_y
     grad_v[H_Y:16, :] = sum_z[0:H_Z - 1]
     gradient = grad_v[...]
     scaled = gradient / sum_z[H_Z - 1:H_Z]
-    scaled_v[...] = scaled
-
-    own = y * nz + z
+
+    first_own = y * nz
+    own = first_own + nz - 1
     dirs[own] = scaled.astype(BF16)
-    ag1 = [push(dirs.at[own], dirs.at[own], sa1.at[d - 1], va1.at[d - 1], z_id(d)) for d in range(1, nz)]
-    for copy in ag1:
-        copy.wait_recv()
-    row = pl.ds(y * nz, nz)
-    ag2 = [push(dirs.at[row], dirs.at[row], sa2.at[d - 1], va2.at[d - 1], y_id(d)) for d in range(1, ny)]
+    ag1 = {d: push(dirs.at[own], dirs.at[first_own + place_of(nz - d, nz)], sa1.at[d - 1], va1.at[d - 1], z_id(d))
+           for d in far_first(nz)}
+    ag2 = []
+    for g in reversed(range(GROUPS)):
+        for place in range(g * places_g, (g + 1) * places_g):
+            if rel_of[place]:
+                ag1[nz - rel_of[place]].wait_recv()
+        part = pl.ds(first_own + g * places_g, places_g)
+        for d in far_first(ny):
+            i = (d - 1) * GROUPS + g
+            ag2.append(push(dirs.at[part], dirs.at[part], sa2.at[i], va2.at[i], y_id(d)))
+    place_copy.wait()
     for copy in ag2:
         copy.wait_recv()
-
-    cs_copy.wait()
 
     def image_of(first):
         def one(j, carry):
             r = first + j
             picked = []
             for k in range(slots):
-                c = cols_s[k, r]
-                picked.append(dirs[(c % ny) * nz + c // ny])
+                picked.append(dirs[place_s[k, r]])
             left = jnp.concatenate(picked, axis=1)
             right = jnp.concatenate([a_v[r, k] for k in range(slots)], axis=1)
             out = lax.dot_general(left, right, (((1,), (1,)), ((), ())), preferred_element_type=F32)
@@ -224,7 +262,6 @@
     nsrc[0] = jnp.sum(squares.T, axis=0, keepdims=True)
     n1 = [push(nsrc.at[0], n1_r.at[i], sn1.at[i], vn1.at[i], zc_id(i)) for i in range(2 * nz - 1)]
     ag_i = [push(img.at[mine], img.at[mine], sg.at[d - 1], vg.at[d - 1], mp_id(d)) for d in range(1, nmp)]
-    it_copy.wait()
     for copy in n1:
         copy.wait_recv()
     acc = nsrc[0]
@@ -239,6 +276,8 @@
           for i in range(1, nx * ny)]
     for copy in ag_i:
         copy.wait_recv()
+    out_copy = pltpu.make_async_copy(img, img_hbm, out_sem)
+    out_copy.start()
     for copy in n2:
         copy.wait_recv()
     acc = n2_r[0]
@@ -250,10 +289,17 @@
     image_norm = jnp.sum(jnp.where(lane16 == sub, wide, 0.0), axis=1, keepdims=True)
     grad_norm = jnp.sum(jnp.where(lane16 == sub + 16, wide, 0.0), axis=1, keepdims=True)
     step = grad_norm / (image_norm + eps)
-    itn_ref[0, 0] = it_v[0, 0] + step * scaled_v[...]
-    resn_ref[...] = res_v[...] - step[None] * img[...]
+    small_ref[0] = scaled
+    small_ref[1] = jnp.broadcast_to(step, (16, 128))
+    out_copy.wait()
     for copy in sends:
         copy.wait_send()
+
+
+def update(small_ref, img_ref, it_ref, res_ref, itn_ref, resn_ref):
+    step = small_ref[1]
+    itn_ref[0, 0] = it_ref[0, 0] + step * small_ref[0]
+    resn_ref[...] = res_ref[...] - step[None] * img_ref[...]
 
 
 def local(ray_matrix, block_cols, iterate, residual):
@@ -267,7 +313,7 @@
     scratch = [
         pltpu.VMEM(ray_matrix.shape, BF16),
         pltpu.VMEM(residual.shape, F32),
-        pltpu.VMEM(iterate.shape, F32),
+        pltpu.VMEM((slots, rb), jnp.int32),
         pltpu.VMEM((slots, rb), jnp.int32),
         pltpu.SMEM((slots, rb), jnp.int32),
         vmem(24 * rb * slots, 128),
@@ -279,7 +325,6 @@
         vmem(NY, 8, 128),
         vmem(nz - 1, 16, 128),
         vmem(NY - 1, 8, 128),
-        vmem(16, 128),
         vmem(16, 128),
         pltpu.VMEM((mb, 16, 128), BF16),
         vmem(rb, 16, 128),
@@ -293,23 +338,36 @@
     ]
     y, z, m = NY - 1, nz - 1, nmp - 1
     zc, yx = 2 * nz - 1, nmp // 2 * NY - 1
-    for n in (y, z, y, z, z, y, z, y, z, z, y, y, m, m, m, m, zc, zc, yx, yx):
+    yg = y * GROUPS
+    for n in (yg, z, yg, z, z, y, z, y, z, z, yg, yg, m, m, m, m, zc, zc, yx, yx):
         scratch.append(dma(n))
     any_spec = pl.BlockSpec(memory_space=pl.ANY)
-    return pl.pallas_call(
+    small, img = pl.pallas_call(
         functools.partial(kernel, nz, nmp),
         out_shape=(
-            jax.ShapeDtypeStruct(iterate.shape, F32),
+            jax.ShapeDtypeStruct((2, 16, 128), F32),
             jax.ShapeDtypeStruct(residual.shape, F32),
         ),
-        in_specs=[any_spec] * 4,
-        out_specs=(pl.BlockSpec(memory_space=pltpu.VMEM),) * 2,
+        in_specs=[any_spec] * 3,
+        out_specs=(pl.BlockSpec(memory_space=pltpu.VMEM), any_spec),
         scratch_shapes=scratch,
         compiler_params=pltpu.CompilerParams(
             collective_id=0, has_side_effects=True, vmem_limit_bytes=61 * 2**20),
         cost_estimate=pl.CostEstimate(flops=300_000_000, bytes_accessed=5_000_000, transcendentals=0),
         name="cgls",
-    )(ray_matrix, block_cols.T, iterate, residual)
+    )(ray_matrix, block_cols.T, residual)
+    return pl.pallas_call(
+        update,
+        out_shape=(
+            jax.ShapeDtypeStruct(iterate.shape, F32),
+            jax.ShapeDtypeStruct(residual.shape, F32),
+        ),
+        in_specs=[pl.BlockSpec(memory_space=pltpu.VMEM)] * 4,
+        out_specs=(pl.BlockSpec(memory_space=pltpu.VMEM),) * 2,
+        compiler_params=pltpu.CompilerParams(vmem_limit_bytes=61 * 2**20),
+        cost_estimate=pl.CostEstimate(flops=200_000, bytes_accessed=800_000, transcendentals=0),
+        name="update",
+    )(small, img, iterate, residual)
 
 
 def solution(mesh):

time: 79.7 us -> 73.7 us (0.925)
  local copies, waits for them, and re-layouts: 2.96 us -> 0 us
  Pallas kernels: 75.8 us -> 72.9 us
    pallas_call x1, Pallas kernels: 75.8 us -> 71.1 us  [local(): pl.pallas_call(functools.partial(kernel, nz, nmp), out_shape=(jax.ShapeDt...]
    unnamed x2 -> x0, local copies, waits for them, and re-layouts: 2.96 us -> none
    pallas_call x0 -> x1, Pallas kernels: none -> 1.8 us  [local(): pl.pallas_call(update, out_shape=(jax.ShapeDtypeStruct(iterate.shape, F32...]
where the time goes in v3:
time: 73.7 us; the launch traced here: 73.5 us
  Pallas kernels  72.9 us (99%)
    pallas_call x1, Pallas kernels, local(): pl.pallas_call(functools.partial(kernel, nz, nmp), out_shape=(jax.ShapeDt...  71.1 us
    pallas_call x1, Pallas kernels, local(): pl.pallas_call(update, out_shape=(jax.ShapeDtypeStruct(iterate.shape, F32...  1.8 us

profile of v3, /device:TPU:1, one launch (start us, length us, event | category | flops | bytes accessed | tf_op | source)
XLA Modules:
  0.0 73.5 jit_solution(1641032683440513280)
XLA Ops:
  0.6 71.1 %cgls.1 = (f32[2,16,128]{2,1,0:T(8,128)}, f32[32,16,128]{2,1,0:T(8,128)}) custom-call(bf16[32,4,128,128]{3,2,1,0:T(8,128)(2,1)} %a_hbm.1, s32[4,32]{1,0:T(4,128)} %bitcast.1, f32[32,16,128]{2,1,0:T(8,128)} %res_ref.1), custom_call_target="tpu_custom_call" | custom-call | flops 300000000 | bytes 5000000 | tf_op jit(solution)/shard_map/cgls/pallas_call | solution.py:345
  71.7 1.8 %update.1 = (f32[1,1,16,128]{3,2,1,0:T(8,128)}, f32[32,16,128]{2,1,0:T(8,128)}) custom-call(f32[2,16,128]{2,1,0:T(8,128)} %get-tuple-element.4.small_ref, f32[32,16,128]{2,1,0:T(8,128)} %get-tuple-element.5.img_ref, f32[1,1,16,128]{3,2,1,0:T(8,128)} %it_ref.1, f32[32,16,128]{2,1,0:T(8,128)} %res_ref.1), custom_call_target="tpu_custom_call" | custom-call | flops 200000 | bytes 800000 | tf_op jit(solution)/shard_map/update/pallas_call | solution.py:359

commit v4 on v3

--- a/solution.py
+++ b/solution.py
@@ -12,10 +12,14 @@
 eps = 1e-06
 
 NY = 8
-H_Y = 10
-H_Z = 7
+H_Y = 11
+H_Z = 6
+PAD = 16
 CHUNKS = 8
-GROUPS = 3
+RS_CUTS = (0, 8)
+AG_CUTS = (0, 3, 7)
+
+RS_Z, RS_Y, RS_Z2, RS_Y2, AG_1, AG_2, RS_I, AG_I, N_1, N_2, PHASES = 0, 1, 3, 4, 5, 8, 9, 10, 11, 12, 13
 
 
 def far_first(n):
@@ -30,8 +34,7 @@
            a_v, res_v, cols_v, place_v, place_s, terms, gy, gz, ry, rz, s2y, s2z, ry2, rz2, grad_v,
            dirs, img_f, img_b, ri, img, nsrc, n1_r, n2_r,
            a_sem, res_sem, cv_sem, ps_sem, out_sem,
-           sy, sz, vy, vz, sy2, sz2, vy2, vz2, sa1, va1, sa2, va2,
-           si, vi, sg, vg, sn1, vn1, sn2, vn2):
+           send_sem, recv_sem):
     ny = NY
     mb = nz * ny
     rb = a_v.shape[0]
@@ -43,15 +46,15 @@
     y = me % ny
     y_of = [None] + [(y + d) % ny for d in range(1, ny)]
     z_of = [None] + [(z + d) % nz for d in range(1, nz)]
-    mp_of = [None] + [(mp + d) % nmp for d in range(1, nmp)]
     y_id = lambda d: (z * ny + y_of[d], mp)
     z_id = lambda d: (z_of[d] * ny + y, mp)
-    mp_id = lambda d: (me, mp_of[d])
 
     nx = nmp // 2
     x = mp // 2
     core = mp % 2
     other_core = x * 2 + 1 - core
+    mp_of = [((x + d) % nx) * 2 + c for d in far_first(nx) for c in (core, 1 - core)] + [other_core]
+    mp_id = lambda i: (me, mp_of[i])
 
     def zc_id(i):
         if i < nz - 1:
@@ -61,20 +64,6 @@
 
     def yx_id(i):
         return (z * ny + (y + i % ny) % ny, ((x + i // ny) % nx) * 2 + core)
-
-    barrier = pltpu.get_barrier_semaphore()
-    for d in far_first(nz):
-        pl.semaphore_signal(barrier, inc=1, device_id=z_id(d), device_id_type=MESH)
-    for d in far_first(ny):
-        pl.semaphore_signal(barrier, inc=1, device_id=y_id(d), device_id_type=MESH)
-    for d in range(1, nmp):
-        pl.semaphore_signal(barrier, inc=1, device_id=mp_id(d), device_id_type=MESH)
-    for i in range(nz, 2 * nz - 1):
-        pl.semaphore_signal(barrier, inc=1, device_id=zc_id(i), device_id_type=MESH)
-    for i in range(ny, nx * ny):
-        if i % ny:
-            pl.semaphore_signal(barrier, inc=1, device_id=yx_id(i), device_id_type=MESH)
-    greeted = (nz - 1) + (ny - 1) + (nmp - 1) + (nz - 1) + (nx - 1) * (ny - 1)
 
     cv_copy = pltpu.make_async_copy(cols_hbm, cols_v, cv_sem)
     cv_copy.start()
@@ -87,20 +76,40 @@
         copy.start()
         a_copies.append(copy)
 
-    sends = []
-
-    def push(src, dst, send_sem, recv_sem, target):
-        copy = pltpu.make_async_remote_copy(
-            src_ref=src, dst_ref=dst, send_sem=send_sem, recv_sem=recv_sem,
-            device_id=target, device_id_type=MESH)
-        copy.start()
-        sends.append(copy)
-        return copy
-
-    block = lax.broadcasted_iota(jnp.int32, (mb, rb), 0)
+    barrier = pltpu.get_barrier_semaphore()
+    for d in far_first(nz):
+        pl.semaphore_signal(barrier, inc=1, device_id=z_id(d), device_id_type=MESH)
+    for d in far_first(ny):
+        pl.semaphore_signal(barrier, inc=1, device_id=y_id(d), device_id_type=MESH)
+    for d in range(nmp - 1):
+        pl.semaphore_signal(barrier, inc=1, device_id=mp_id(d), device_id_type=MESH)
+    for i in range(nz, 2 * nz - 1):
+        pl.semaphore_signal(barrier, inc=1, device_id=zc_id(i), device_id_type=MESH)
+    for i in range(ny, nx * ny):
+        if i % ny:
+            pl.semaphore_signal(barrier, inc=1, device_id=yx_id(i), device_id_type=MESH)
+    greeted = (nz - 1) + (ny - 1) + (nmp - 1) + (nz - 1) + (nx - 1) * (ny - 1)
+
+    def push(src, dst, phase, target, group=0):
+        pltpu.make_async_remote_copy(
+            src_ref=src, dst_ref=dst, send_sem=send_sem.at[phase], recv_sem=recv_sem.at[phase + group],
+            device_id=target, device_id_type=MESH).start()
+
+    def all_of(ref, phase, group=0):
+        return pltpu.make_async_remote_copy(
+            src_ref=ref, dst_ref=ref, send_sem=send_sem.at[phase], recv_sem=recv_sem.at[phase + group],
+            device_id=y_id(1), device_id_type=MESH)
+
+    def received(ref, phase, group=0):
+        all_of(ref, phase, group).wait_recv()
+
+    def sent(ref, phase):
+        all_of(ref, phase).wait_send()
+
     slots = cols_v.shape[0]
 
-    def one_hot(place):
+    def one_hot(blocks, place):
+        block = lax.broadcasted_iota(jnp.int32, (blocks, rb), 0)
         parts = [(place(cols_v[k:k + 1, :]) == block).astype(F32) for k in range(slots)]
         hot = jnp.concatenate(parts, axis=1).astype(BF16)
         return jnp.concatenate([hot, hot, hot], axis=1)
@@ -112,11 +121,10 @@
         rel = jnp.where(rel < 0, rel + n, rel)
         return jnp.where(rel < n // 2, n - 1 - 2 * rel, 2 * rel - n)
 
-    place_z = lambda c: (c // ny) * ny + near(c % ny, y, ny)
-    place_y = lambda c: (c % ny) * nz + near(c // ny, z, nz)
-    hot_z = one_hot(place_z)
-    hot_y = one_hot(place_y)
-    place_v[...] = place_y(cols_v[...])
+    near_z = lambda c: near(c // ny, z, nz)
+    hot_z = one_hot(mb, lambda c: (c // ny) * ny + near(c % ny, y, ny))
+    hot_y = one_hot(ny * PAD, lambda c: (c % ny) * PAD + near_z(c))
+    place_v[...] = (cols_v[...] % ny) * nz + near_z(cols_v[...])
     place_copy = pltpu.make_async_copy(place_v, place_s, ps_sem)
     place_copy.start()
 
@@ -151,60 +159,56 @@
             right = jnp.concatenate([split(first + h + i) for i in range(n)], axis=1)
             out = jnp.dot(hot, right, preferred_element_type=F32)
             for i in range(n):
-                dst[pl.ds(h + i, mb, stride=rows), :] = out[:, i * 128:(i + 1) * 128]
+                dst[pl.ds(h + i, hot.shape[0], stride=rows), :] = out[:, i * 128:(i + 1) * 128]
 
     segment(hot_z, gz, H_Z, H_Y)
     pl.semaphore_wait(barrier, greeted)
     len_z = ny * H_Z
-    len_y = nz * H_Y
-    rs_z = {d: push(gz.at[pl.ds(z_of[d] * len_z, len_z)], rz.at[d - 1], sz.at[d - 1], vz.at[d - 1], z_id(d))
-            for d in far_first(nz)}
+    len_y = PAD * H_Y
+    for d in far_first(nz):
+        push(gz.at[pl.ds(z_of[d] * len_z, len_z)], rz.at[d - 1], RS_Z, z_id(d))
     segment(hot_y, gy, H_Y, 0)
-    len_g = len_y // GROUPS
-    places_g = nz // GROUPS
-    rs_y = {}
-    for g in range(GROUPS):
+    groups = list(zip(RS_CUTS, RS_CUTS[1:] + (nz,)))
+    rows_of = lambda low, high: pl.ds(low * H_Y, -(-(high - low) * H_Y // 8) * 8)
+    for g, (low, high) in enumerate(groups):
+        rows = rows_of(low, high)
         for d in far_first(ny):
-            i = (d - 1) * GROUPS + g
-            rs_y[d, g] = push(gy.at[pl.ds(y_of[d] * len_y + g * len_g, len_g)],
-                              ry.at[d - 1, pl.ds(g * len_g, len_g)], sy.at[i], vy.at[i], y_id(d))
+            push(gy.at[pl.ds(y_of[d] * len_y + rows.start, rows.size)], ry.at[d - 1, rows], RS_Y, y_id(d), g)
     rel_of = {place_of(rel, nz): rel for rel in range(nz)}
-    rs_y2 = {}
 
     def sum_group(g):
-        part = gy[pl.ds(pl.multiple_of(y * len_y + g * len_g, 8), len_g), :]
-        for d in far_first(ny):
-            rs_y[d, g].wait_recv()
+        low, high = groups[g]
+        rows = rows_of(low, high)
+        part = gy[pl.ds(pl.multiple_of(y * len_y + rows.start, 8), rows.size), :]
+        received(ry.at[:, rows], RS_Y, g)
         for d in range(1, ny):
-            part = part + ry[d - 1, g * len_g:(g + 1) * len_g]
-        for i in range(places_g):
-            place = g * places_g + i
+            part = part + ry[d - 1, rows]
+        for i in range(high - low):
+            place = low + i
             s2y[place, 0:H_Y, :] = part[i * H_Y:(i + 1) * H_Y]
             d = rel_of[place]
             if d:
-                rs_y2[d] = push(s2y.at[place, pl.ds(0, H_Y)], ry2.at[d - 1, pl.ds(0, H_Y)],
-                                sy2.at[d - 1], vy2.at[d - 1], z_id(d))
-
-    for g in range(GROUPS - 1):
+                push(s2y.at[place, pl.ds(0, H_Y)], ry2.at[d - 1, pl.ds(0, H_Y)], RS_Y2, z_id(d))
+
+    for g in range(len(groups) - 1):
         sum_group(g)
     acc_z = gz[pl.ds(pl.multiple_of(z * len_z, 8), len_z), :]
-    for d in far_first(nz):
-        rs_z[d].wait_recv()
+    received(rz, RS_Z)
     for d in range(1, nz):
         acc_z = acc_z + rz[d - 1]
     for i in range(ny):
         s2z[i, 0:H_Z, :] = acc_z[i * H_Z:(i + 1) * H_Z]
-    rs_z2 = {d: push(s2z.at[place_of(d, ny)], rz2.at[d - 1], sz2.at[d - 1], vz2.at[d - 1], y_id(d))
-             for d in far_first(ny)}
-    sum_group(GROUPS - 1)
+    for d in far_first(ny):
+        push(s2z.at[place_of(d, ny)], rz2.at[d - 1], RS_Z2, y_id(d))
+    sum_group(len(groups) - 1)
 
     sum_z = s2z[ny - 1]
+    received(rz2, RS_Z2)
     for d in range(1, ny):
-        rs_z2[d].wait_recv()
         sum_z = sum_z + rz2[d - 1]
     sum_y = s2y[nz - 1, 0:H_Y]
+    received(ry2.at[:, pl.ds(0, H_Y)], RS_Y2)
     for d in range(1, nz):
-        rs_y2[d].wait_recv()
         sum_y = sum_y + ry2[d - 1, 0:H_Y]
     grad_v[0:H_Y, :] = sum_y
     grad_v[H_Y:16, :] = sum_z[0:H_Z - 1]
@@ -214,20 +218,23 @@
     first_own = y * nz
     own = first_own + nz - 1
     dirs[own] = scaled.astype(BF16)
-    ag1 = {d: push(dirs.at[own], dirs.at[first_own + place_of(nz - d, nz)], sa1.at[d - 1], va1.at[d - 1], z_id(d))
-           for d in far_first(nz)}
-    ag2 = []
-    for g in reversed(range(GROUPS)):
-        for place in range(g * places_g, (g + 1) * places_g):
-            if rel_of[place]:
-                ag1[nz - rel_of[place]].wait_recv()
-        part = pl.ds(first_own + g * places_g, places_g)
+    cuts = list(zip(AG_CUTS, AG_CUTS[1:] + (nz,)))
+    for d in far_first(nz):
+        place = place_of(nz - d, nz)
+        group = max(g for g, (low, high) in enumerate(cuts) if low <= place)
+        push(dirs.at[own], dirs.at[first_own + place], AG_1, z_id(d), group)
+    sent(rz, RS_Z)
+    sent(ry.at[:, pl.ds(0, sum(rows_of(low, high).size for low, high in groups))], RS_Y)
+    sent(rz2, RS_Z2)
+    sent(ry2.at[:, pl.ds(0, H_Y)], RS_Y2)
+    for g, (low, high) in reversed(list(enumerate(cuts))):
+        received(dirs.at[pl.ds(first_own + low, min(high, nz - 1) - low)], AG_1, g)
+        part = pl.ds(first_own + low, high - low)
         for d in far_first(ny):
-            i = (d - 1) * GROUPS + g
-            ag2.append(push(dirs.at[part], dirs.at[part], sa2.at[i], va2.at[i], y_id(d)))
+            push(dirs.at[part], dirs.at[part], AG_2, y_id(d))
     place_copy.wait()
-    for copy in ag2:
-        copy.wait_recv()
+    sent(dirs.at[pl.ds(0, nz - 1)], AG_1)
+    received(dirs.at[pl.ds(0, mb - nz)], AG_2)
 
     def image_of(first):
         def one(j, carry):
@@ -244,26 +251,28 @@
 
         lax.fori_loop(0, rb_own, one, 0, unroll=True)
 
-    rs_i = []
-    for d in range(1, nmp):
-        first = mp_of[d] * rb_own
+    for i in range(nmp - 1):
+        first = mp_of[i] * rb_own
         image_of(first)
-        rs_i.append(push(img_b.at[pl.ds(first, rb_own)], ri.at[d - 1], si.at[d - 1], vi.at[d - 1], mp_id(d)))
+        push(img_b.at[pl.ds(first, rb_own)], ri.at[i], RS_I, mp_id(i))
     mine = pl.ds(mp * rb_own, rb_own)
     image_of(mp * rb_own)
     total = img_f[mine]
-    for d in range(1, nmp):
-        rs_i[d - 1].wait_recv()
-        total = total + ri[d - 1].astype(F32)
+    received(ri, RS_I)
+    for i in range(nmp - 1):
+        total = total + ri[i].astype(F32)
     img[mine] = total
 
     squares = jnp.concatenate(
         [jnp.sum(total * total, axis=0), gradient * scaled, jnp.zeros((96, 128), F32)], axis=0)
     nsrc[0] = jnp.sum(squares.T, axis=0, keepdims=True)
-    n1 = [push(nsrc.at[0], n1_r.at[i], sn1.at[i], vn1.at[i], zc_id(i)) for i in range(2 * nz - 1)]
-    ag_i = [push(img.at[mine], img.at[mine], sg.at[d - 1], vg.at[d - 1], mp_id(d)) for d in range(1, nmp)]
-    for copy in n1:
-        copy.wait_recv()
+    for i in range(2 * nz - 1):
+        push(nsrc.at[0], n1_r.at[i], N_1, zc_id(i))
+    for i in range(nmp - 1):
+        push(img.at[mine], img.at[mine], AG_I, mp_id(i))
+    sent(dirs.at[pl.ds(0, mb - nz)], AG_2)
+    sent(ri, RS_I)
+    received(n1_r, N_1)
     acc = nsrc[0]
     for i in range(nz - 1):
         acc = acc + n1_r[i]
@@ -272,14 +281,14 @@
         other = other + n1_r[i]
     own_x = pl.ds(x * ny, 1)
     n2_r[own_x] = (acc + other)[None]
-    n2 = [push(n2_r.at[own_x], n2_r.at[pl.ds(x * ny + i % ny, 1)], sn2.at[i - 1], vn2.at[i - 1], yx_id(i))
-          for i in range(1, nx * ny)]
-    for copy in ag_i:
-        copy.wait_recv()
+    for i in range(1, nx * ny):
+        push(n2_r.at[own_x], n2_r.at[pl.ds(x * ny + i % ny, 1)], N_2, yx_id(i))
+    sent(n1_r, N_1)
+    received(img.at[pl.ds(0, rb - rb_own)], AG_I)
     out_copy = pltpu.make_async_copy(img, img_hbm, out_sem)
     out_copy.start()
-    for copy in n2:
-        copy.wait_recv()
+    sent(img.at[pl.ds(0, rb - rb_own)], AG_I)
+    received(n2_r.at[pl.ds(0, nx * ny - 1)], N_2)
     acc = n2_r[0]
     for i in range(1, nx * ny):
         acc = acc + n2_r[i]
@@ -292,8 +301,7 @@
     small_ref[0] = scaled
     small_ref[1] = jnp.broadcast_to(step, (16, 128))
     out_copy.wait()
-    for copy in sends:
-        copy.wait_send()
+    sent(n2_r.at[pl.ds(0, nx * ny - 1)], N_2)
 
 
 def update(small_ref, img_ref, it_ref, res_ref, itn_ref, resn_ref):
@@ -317,9 +325,9 @@
         pltpu.VMEM((slots, rb), jnp.int32),
         pltpu.SMEM((slots, rb), jnp.int32),
         vmem(24 * rb * slots, 128),
-        vmem(mb * H_Y, 128),
+        vmem(NY * PAD * H_Y, 128),
         vmem(mb * H_Z, 128),
-        vmem(NY - 1, nz * H_Y, 128),
+        vmem(NY - 1, PAD * H_Y, 128),
         vmem(nz - 1, NY * H_Z, 128),
         vmem(nz, 16, 128),
         vmem(NY, 8, 128),
@@ -336,11 +344,7 @@
         vmem(nmp // 2 * NY, 1, 128),
         dma(CHUNKS), *[pltpu.SemaphoreType.DMA] * 4,
     ]
-    y, z, m = NY - 1, nz - 1, nmp - 1
-    zc, yx = 2 * nz - 1, nmp // 2 * NY - 1
-    yg = y * GROUPS
-    for n in (yg, z, yg, z, z, y, z, y, z, z, yg, yg, m, m, m, m, zc, zc, yx, yx):
-        scratch.append(dma(n))
+    scratch += [dma(PHASES), dma(PHASES)]
     any_spec = pl.BlockSpec(memory_space=pl.ANY)
     small, img = pl.pallas_call(
         functools.partial(kernel, nz, nmp),

time: 73.7 us -> 70.4 us (0.955)
  Pallas kernels: 72.9 us -> 69.6 us
    pallas_call x1, Pallas kernels: 71.1 us -> 67.8 us  [local(): pl.pallas_call(functools.partial(kernel, nz, nmp), out_shape=(jax.ShapeDt...]
where the time goes in v4:
time: 70.4 us; the launch traced here: 70.2 us
  Pallas kernels  69.6 us (99%)
    pallas_call x1, Pallas kernels, local(): pl.pallas_call(functools.partial(kernel, nz, nmp), out_shape=(jax.ShapeDt...  67.8 us
    pallas_call x1, Pallas kernels, local(): pl.pallas_call(update, out_shape=(jax.ShapeDtypeStruct(iterate.shape, F32...  1.8 us

profile of v4, /device:TPU:1, one launch (start us, length us, event | category | flops | bytes accessed | tf_op | source)
XLA Modules:
  0.0 70.2 jit_solution(710359833424824939)
XLA Ops:
  0.6 67.8 %cgls.1 = (f32[2,16,128]{2,1,0:T(8,128)}, f32[32,16,128]{2,1,0:T(8,128)}) custom-call(bf16[32,4,128,128]{3,2,1,0:T(8,128)(2,1)} %a_hbm.1, s32[4,32]{1,0:T(4,128)} %bitcast.1, f32[32,16,128]{2,1,0:T(8,128)} %res_ref.1), custom_call_target="tpu_custom_call" | custom-call | flops 300000000 | bytes 5000000 | tf_op jit(solution)/shard_map/cgls/pallas_call | solution.py:349
  68.4 1.8 %update.1 = (f32[1,1,16,128]{3,2,1,0:T(8,128)}, f32[32,16,128]{2,1,0:T(8,128)}) custom-call(f32[2,16,128]{2,1,0:T(8,128)} %get-tuple-element.4.small_ref, f32[32,16,128]{2,1,0:T(8,128)} %get-tuple-element.5.img_ref, f32[1,1,16,128]{3,2,1,0:T(8,128)} %it_ref.1, f32[32,16,128]{2,1,0:T(8,128)} %res_ref.1), custom_call_target="tpu_custom_call" | custom-call | flops 200000 | bytes 800000 | tf_op jit(solution)/shard_map/update/pallas_call | solution.py:363

commit v5 on v4

--- a/solution.py
+++ b/solution.py
@@ -14,12 +14,14 @@
 NY = 8
 H_Y = 11
 H_Z = 6
-PAD = 16
 CHUNKS = 8
-RS_CUTS = (0, 8)
+RS_CUTS = (0, 4, 9)
+STRIDE = 8
+RZ_CUTS = (0, 4)
 AG_CUTS = (0, 3, 7)
 
-RS_Z, RS_Y, RS_Z2, RS_Y2, AG_1, AG_2, RS_I, AG_I, N_1, N_2, PHASES = 0, 1, 3, 4, 5, 8, 9, 10, 11, 12, 13
+RS_Z, RS_Y, RS_Z2, RS_Y2, AG_1, AG_2, RS_I, AG_I, N_1, N_2, PHASES = 0, 2, 5, 6, 7, 10, 11, 12, 13, 14, 15
+PAD = STRIDE * len(RS_CUTS)
 
 
 def far_first(n):
@@ -122,8 +124,13 @@
         return jnp.where(rel < n // 2, n - 1 - 2 * rel, 2 * rel - n)
 
     near_z = lambda c: near(c // ny, z, nz)
+
+    def spot(place):
+        return place + sum(
+            jnp.where(place >= low, STRIDE - low + last, 0) for last, low in zip(RS_CUTS, RS_CUTS[1:]))
+
     hot_z = one_hot(mb, lambda c: (c // ny) * ny + near(c % ny, y, ny))
-    hot_y = one_hot(ny * PAD, lambda c: (c % ny) * PAD + near_z(c))
+    hot_y = one_hot(ny * PAD, lambda c: (c % ny) * PAD + spot(near_z(c)))
     place_v[...] = (cols_v[...] % ny) * nz + near_z(cols_v[...])
     place_copy = pltpu.make_async_copy(place_v, place_s, ps_sem)
     place_copy.start()
@@ -161,24 +168,28 @@
             for i in range(n):
                 dst[pl.ds(h + i, hot.shape[0], stride=rows), :] = out[:, i * 128:(i + 1) * 128]
 
-    segment(hot_z, gz, H_Z, H_Y)
+    segment(hot_y, gy, H_Y, 0)
     pl.semaphore_wait(barrier, greeted)
     len_z = ny * H_Z
     len_y = PAD * H_Y
-    for d in far_first(nz):
-        push(gz.at[pl.ds(z_of[d] * len_z, len_z)], rz.at[d - 1], RS_Z, z_id(d))
-    segment(hot_y, gy, H_Y, 0)
     groups = list(zip(RS_CUTS, RS_CUTS[1:] + (nz,)))
-    rows_of = lambda low, high: pl.ds(low * H_Y, -(-(high - low) * H_Y // 8) * 8)
-    for g, (low, high) in enumerate(groups):
-        rows = rows_of(low, high)
+    rows_of = lambda g: pl.ds(g * STRIDE * H_Y, (groups[g][1] - groups[g][0]) * H_Y)
+    groups_z = list(zip(RZ_CUTS, RZ_CUTS[1:] + (ny,)))
+    rows_z = lambda g: pl.ds(groups_z[g][0] * H_Z, (groups_z[g][1] - groups_z[g][0]) * H_Z)
+    for g in range(len(groups)):
+        rows = rows_of(g)
         for d in far_first(ny):
             push(gy.at[pl.ds(y_of[d] * len_y + rows.start, rows.size)], ry.at[d - 1, rows], RS_Y, y_id(d), g)
+    segment(hot_z, gz, H_Z, H_Y)
+    for g in range(len(groups_z)):
+        rows = rows_z(g)
+        for d in far_first(nz):
+            push(gz.at[pl.ds(z_of[d] * len_z + rows.start, rows.size)], rz.at[d - 1, rows], RS_Z, z_id(d), g)
     rel_of = {place_of(rel, nz): rel for rel in range(nz)}
 
     def sum_group(g):
         low, high = groups[g]
-        rows = rows_of(low, high)
+        rows = rows_of(g)
         part = gy[pl.ds(pl.multiple_of(y * len_y + rows.start, 8), rows.size), :]
         received(ry.at[:, rows], RS_Y, g)
         for d in range(1, ny):
@@ -190,17 +201,27 @@
             if d:
                 push(s2y.at[place, pl.ds(0, H_Y)], ry2.at[d - 1, pl.ds(0, H_Y)], RS_Y2, z_id(d))
 
-    for g in range(len(groups) - 1):
-        sum_group(g)
-    acc_z = gz[pl.ds(pl.multiple_of(z * len_z, 8), len_z), :]
-    received(rz, RS_Z)
-    for d in range(1, nz):
-        acc_z = acc_z + rz[d - 1]
-    for i in range(ny):
-        s2z[i, 0:H_Z, :] = acc_z[i * H_Z:(i + 1) * H_Z]
-    for d in far_first(ny):
-        push(s2z.at[place_of(d, ny)], rz2.at[d - 1], RS_Z2, y_id(d))
-    sum_group(len(groups) - 1)
+    rel_z = {place_of(rel, ny): rel for rel in range(ny)}
+
+    def sum_group_z(g):
+        low, high = groups_z[g]
+        rows = rows_z(g)
+        part = gz[pl.ds(pl.multiple_of(z * len_z + rows.start, 8), rows.size), :]
+        received(rz.at[:, rows], RS_Z, g)
+        for d in range(1, nz):
+            part = part + rz[d - 1, rows]
+        for i in range(high - low):
+            place = low + i
+            s2z[place, 0:H_Z, :] = part[i * H_Z:(i + 1) * H_Z]
+            d = rel_z[place]
+            if d:
+                push(s2z.at[place], rz2.at[d - 1], RS_Z2, y_id(d))
+
+    sum_group(0)
+    sum_group_z(0)
+    sum_group(1)
+    sum_group_z(1)
+    sum_group(2)
 
     sum_z = s2z[ny - 1]
     received(rz2, RS_Z2)
@@ -224,7 +245,7 @@
         group = max(g for g, (low, high) in enumerate(cuts) if low <= place)
         push(dirs.at[own], dirs.at[first_own + place], AG_1, z_id(d), group)
     sent(rz, RS_Z)
-    sent(ry.at[:, pl.ds(0, sum(rows_of(low, high).size for low, high in groups))], RS_Y)
+    sent(ry.at[:, pl.ds(0, nz * H_Y)], RS_Y)
     sent(rz2, RS_Z2)
     sent(ry2.at[:, pl.ds(0, H_Y)], RS_Y2)
     for g, (low, high) in reversed(list(enumerate(cuts))):

time: 70.4 us -> 69.4 us (0.986)
  Pallas kernels: 69.6 us -> 68.6 us
    pallas_call x1, Pallas kernels: 67.8 us -> 66.8 us  [local(): pl.pallas_call(functools.partial(kernel, nz, nmp), out_shape=(jax.ShapeDt...]
where the time goes in v5:
time: 69.4 us; the launch traced here: 69.2 us
  Pallas kernels  68.6 us (99%)
    pallas_call x1, Pallas kernels, local(): pl.pallas_call(functools.partial(kernel, nz, nmp), out_shape=(jax.ShapeDt...  66.8 us
    pallas_call x1, Pallas kernels, local(): pl.pallas_call(update, out_shape=(jax.ShapeDtypeStruct(iterate.shape, F32...  1.8 us

profile of v5, /device:TPU:1, one launch (start us, length us, event | category | flops | bytes accessed | tf_op | source)
XLA Modules:
  0.0 69.2 jit_solution(3532189276785494729)
XLA Ops:
  0.6 66.8 %cgls.1 = (f32[2,16,128]{2,1,0:T(8,128)}, f32[32,16,128]{2,1,0:T(8,128)}) custom-call(bf16[32,4,128,128]{3,2,1,0:T(8,128)(2,1)} %a_hbm.1, s32[4,32]{1,0:T(4,128)} %bitcast.1, f32[32,16,128]{2,1,0:T(8,128)} %res_ref.1), custom_call_target="tpu_custom_call" | custom-call | flops 300000000 | bytes 5000000 | tf_op jit(solution)/shard_map/cgls/pallas_call | solution.py:370
  67.4 1.8 %update.1 = (f32[1,1,16,128]{3,2,1,0:T(8,128)}, f32[32,16,128]{2,1,0:T(8,128)}) custom-call(f32[2,16,128]{2,1,0:T(8,128)} %get-tuple-element.4.small_ref, f32[32,16,128]{2,1,0:T(8,128)} %get-tuple-element.5.img_ref, f32[1,1,16,128]{3,2,1,0:T(8,128)} %it_ref.1, f32[32,16,128]{2,1,0:T(8,128)} %res_ref.1), custom_call_target="tpu_custom_call" | custom-call | flops 200000 | bytes 800000 | tf_op jit(solution)/shard_map/update/pallas_call | solution.py:384

commit v6 on v5

--- a/solution.py
+++ b/solution.py
@@ -233,7 +233,7 @@
         sum_y = sum_y + ry2[d - 1, 0:H_Y]
     grad_v[0:H_Y, :] = sum_y
     grad_v[H_Y:16, :] = sum_z[0:H_Z - 1]
-    gradient = grad_v[...]
+    gradient = grad_v[0:16, :]
     scaled = gradient / sum_z[H_Z - 1:H_Z]
 
     first_own = y * nz
@@ -345,16 +345,16 @@
         pltpu.VMEM((slots, rb), jnp.int32),
         pltpu.VMEM((slots, rb), jnp.int32),
         pltpu.SMEM((slots, rb), jnp.int32),
-        vmem(24 * rb * slots, 128),
-        vmem(NY * PAD * H_Y, 128),
-        vmem(mb * H_Z, 128),
+        vmem(25 * rb * slots, 128),
+        vmem(NY * PAD * H_Y + 16, 128),
+        vmem(mb * H_Z + 16, 128),
         vmem(NY - 1, PAD * H_Y, 128),
         vmem(nz - 1, NY * H_Z, 128),
         vmem(nz, 16, 128),
         vmem(NY, 8, 128),
         vmem(nz - 1, 16, 128),
         vmem(NY - 1, 8, 128),
-        vmem(16, 128),
+        vmem(24, 128),
         pltpu.VMEM((mb, 16, 128), BF16),
         vmem(rb, 16, 128),
         pltpu.VMEM((rb, 16, 128), BF16),

time: 69.4 us -> 69.4 us (level)
  no operation moved by 1% of the time
where the time goes in v6:
time: 69.4 us; the launch traced here: 69.2 us
  Pallas kernels  68.6 us (99%)
    pallas_call x1, Pallas kernels, local(): pl.pallas_call(functools.partial(kernel, nz, nmp), out_shape=(jax.ShapeDt...  66.8 us
    pallas_call x1, Pallas kernels, local(): pl.pallas_call(update, out_shape=(jax.ShapeDtypeStruct(iterate.shape, F32...  1.8 us

profile of v6, /device:TPU:1, one launch (start us, length us, event | category | flops | bytes accessed | tf_op | source)
XLA Modules:
  0.0 69.2 jit_solution(17453321369722414827)
XLA Ops:
  0.6 66.8 %cgls.1 = (f32[2,16,128]{2,1,0:T(8,128)}, f32[32,16,128]{2,1,0:T(8,128)}) custom-call(bf16[32,4,128,128]{3,2,1,0:T(8,128)(2,1)} %a_hbm.1, s32[4,32]{1,0:T(4,128)} %bitcast.1, f32[32,16,128]{2,1,0:T(8,128)} %res_ref.1), custom_call_target="tpu_custom_call" | custom-call | flops 300000000 | bytes 5000000 | tf_op jit(solution)/shard_map/cgls/pallas_call | solution.py:370
  67.4 1.8 %update.1 = (f32[1,1,16,128]{3,2,1,0:T(8,128)}, f32[32,16,128]{2,1,0:T(8,128)}) custom-call(f32[2,16,128]{2,1,0:T(8,128)} %get-tuple-element.4.small_ref, f32[32,16,128]{2,1,0:T(8,128)} %get-tuple-element.5.img_ref, f32[1,1,16,128]{3,2,1,0:T(8,128)} %it_ref.1, f32[32,16,128]{2,1,0:T(8,128)} %res_ref.1), custom_call_target="tpu_custom_call" | custom-call | flops 200000 | bytes 800000 | tf_op jit(solution)/shard_map/update/pallas_call | solution.py:384
